TPU v7x, 32 devices: a whole 2x2x4 slice. The times are simulated.
32 devices in a mesh: grp: 2 (over y), step: 4 (over z), chain: 2 (over x), rep: 2 (over core).
Axes of the slice: x: 2, y: 2, z: 4, core: 2. Of those that a mesh axis runs over, the one named last changes fastest.
Arguments:
- init_seed: int32 [8], P(('grp', 'chain', 'rep')), parts along dimension 0, may hold values from 0 to 63
- noise_index: int32 [8, 32], P(('grp', 'chain', 'rep'), 'step'), parts along dimension 0, may hold values from 0 to 4095
- init_table: float32 [64, 256], replicated, may hold values from -6 to 6
- noise_table: float32 [4096, 256], replicated, may hold values from -6 to 6
- weight: float32 [256, 256], replicated
- bias: float32 [256], replicated, may hold values from -3 to 3
- rates: float32 [64, 256], P(('grp', 'step')), parts along dimension 0, may hold values from 0 to 0.5
- old_path: float32 [8, 32, 256], P(('grp', 'chain', 'rep'), 'step'), parts along dimension 0, may hold values from -6 to 6
- cotangent: float32 [8, 32, 256], P(('grp', 'chain', 'rep'), 'step'), parts along dimension 0, may hold values from -0.3 to 0.3
Outputs:
- path_new: float32 [8, 32, 256], P(('grp', 'chain', 'rep'), 'step'), parts along dimension 0
- grad_w: float32 [512, 256], P('grp'), parts along dimension 0
- grad_b: float32 [512], P('grp'), parts along dimension 0
There are 2 independent parts, one for each index of `grp`. A program takes and returns all parts, laid end to end along the dimension named above; an argument that names none is the same for every part. Nothing has to cross between parts.
All inputs are finite; a program needn't handle non-finite values.
Results may differ from a plain program's by a relative error of at most 0.0001.
Values sent between devices are 32-bit elements; how exact they have to be, the bound alone decides.
A program may use at most 64 MiB of HBM per device.

v0:
```python
import jax
import jax.numpy as jnp
from jax import lax
from jax.sharding import PartitionSpec as P


def shifted_2(block, axis, distance):
    devices = range(lax.axis_size(axis))
    route = [(i - distance, i) for i in devices if i - distance in devices]
    return lax.ppermute(block, axis, route)


def carried_in(x, axis, combine, identity, reverse):
    length, mine = (lax.axis_size(axis), lax.axis_index(axis))
    everything = jax.tree.map(lambda part: lax.all_gather(part, axis), x)
    start = jax.tree.map(
        lambda part, zero: jnp.broadcast_to(jnp.asarray(zero, part.dtype), part.shape), x, identity
    )

    def turn(k, before):
        at = length - 1 - k if reverse else k
        reached = at > mine if reverse else at < mine
        new = combine(before, jax.tree.map(lambda part: part[at], everything))
        return jax.tree.map(lambda a, b: jnp.where(reached, a, b), new, before)

    return lax.fori_loop(0, length, turn, start)


def compose(earlier, later):
    early_mat, early_vec = earlier
    late_mat, late_vec = later
    highest = lax.Precision.HIGHEST
    new_mat = jnp.einsum("...ij,...jk->...ik", late_mat, early_mat, precision=highest)
    new_vec = jnp.einsum("...ij,...j->...i", late_mat, early_vec, precision=highest) + late_vec
    return (new_mat, new_vec)


def shards(
    init_seed, noise_index, init_table, noise_table, weight, bias, rates, old_path, cotangent
):
    highest = lax.Precision.HIGHEST
    chains, steps, width = old_path.shape
    ranks = lax.axis_size("step")
    position = lax.axis_index("step")
    step_size = 4.0 / (steps * ranks)
    start_state = init_table[init_seed]
    shifted = shifted_2(old_path[:, -1], "step", 1)
    first_prev = jnp.where(position == 0, start_state, shifted)
    previous = jnp.concatenate([first_prev[:, None], old_path[:, :-1]], axis=1)
    mixed = jnp.einsum("ctj,ij->cti", previous, weight, precision=highest)
    squash = jnp.tanh(mixed + bias + noise_table[noise_index])
    slope = 1.0 - squash * squash
    keep_rate = 1.0 - rates
    offset = step_size * (squash - slope * mixed)
    identity = jnp.eye(width, dtype=jnp.float32)
    jacobian = keep_rate[None, :, :, None] * identity + step_size * slope[:, :, :, None] * weight
    prefix_mat, prefix_vec = lax.associative_scan(compose, (jacobian, offset), axis=1)
    transposed = jnp.swapaxes(jacobian, 2, 3)
    source = jnp.einsum("ctij,ctj->cti", transposed, cotangent, precision=highest)
    flip_mat, flip_vec = lax.associative_scan(
        compose, (jnp.flip(transposed, 1), jnp.flip(source, 1)), axis=1
    )
    suffix_mat = jnp.flip(flip_mat, 1)
    suffix_vec = jnp.flip(flip_vec, 1)
    block_mat = prefix_mat[:, -1]
    block_vec = prefix_vec[:, -1]
    back_vec = suffix_vec[:, 0]
    neutral = (jnp.broadcast_to(identity, block_mat.shape), jnp.zeros_like(block_vec))
    ahead_mat, ahead_vec = carried_in((block_mat, block_vec), "step", compose, neutral, False)
    entry_state = jnp.einsum("cij,cj->ci", ahead_mat, start_state, precision=highest) + ahead_vec
    behind_mat, adjoint_in = carried_in(
        (suffix_mat[:, 0], back_vec), "step", compose, neutral, True
    )
    path_new = jnp.einsum("ctij,cj->cti", prefix_mat, entry_state, precision=highest) + prefix_vec
    carried = jnp.einsum("ctij,cj->cti", suffix_mat, adjoint_in, precision=highest) + suffix_vec
    following = jnp.concatenate([carried[:, 1:], adjoint_in[:, None]], axis=1)
    adjoint = cotangent + following
    weighted = adjoint * slope
    grad_local = step_size * jnp.einsum("cti,ctj->ij", weighted, previous, precision=highest)
    bias_local = step_size * jnp.sum(weighted, axis=(0, 1))
    grad_w, grad_b = lax.psum((grad_local, bias_local), ("step", "chain", "rep"))
    return (path_new, grad_w, grad_b)


def solution(mesh):
    placed = (
        P(("grp", "chain", "rep")),
        P(("grp", "chain", "rep"), "step"),
        P(),
        P(),
        P(),
        P(),
        P(("grp", "step"), None),
        P(("grp", "chain", "rep"), "step", None),
        P(("grp", "chain", "rep"), "step", None),
    )
    return jax.shard_map(
        shards,
        mesh=mesh,
        in_specs=placed,
        out_specs=(P(("grp", "chain", "rep"), "step", None), P("grp", None), P("grp")),
        check_vma=False,
    )
```

profile of v0, /device:TPU:0, one launch (start us, length us, event | category | flops | bytes accessed | tf_op | source)
XLA Modules:
  0.0 272.2 jit_solution(16754340663512875002)
XLA Ops:
  8.0 4.9 %collective-permute-start = (f32[1,256]{1,0:T(1,128)S(1)}, f32[1,256]{1,0:T(1,128)S(1)}, u32[]{:S(2)}, u32[]{:S(2)}) collective-permute-start(f32[1,256]{1,0:T(1,128)S(1)} %slice_bitcast_fusion.12), channel_id=1, source_target_pairs={{0,4},{4,8},{8,12},{1,5},{5,9},{9,13},{2,6},{6,10},{10,14},{3,7},{... | collective-permute-start | bytes 3080 | tf_op jit(solution)/shard_map/ppermute | solution.py:10
  14.3 2.8 %gather_fusion = f32[8,256]{1,0:T(8,128)S(1)} fusion(f32[4096,256]{1,0:T(8,128)} %param.16, s32[1024]{0:T(1024)S(1)} %pad_clamp_fusion), kind=kCustom, calls=%fused_computation | custom fusion | bytes 16416 | tf_op jit(solution)/shard_map/gather | solution.py:51
  17.7 1.2 fusion.88
  19.8 2.4 fusion.21
  22.4 1.7 fusion.83
  25.9 2.1 slice.222
  28.0 1.5 fusion.121
  29.4 1.3 slice.225
  38.2 2.8 %pad.79 = f32[1,4,256,256]{3,2,1,0:T(8,128)} pad(f32[1,2,256,256]{3,2,1,0:T(8,128)} %pad_add_fusion.1, f32[]{:T(128)} %constant.88.clone.1), padding=0_0_0x1_0_1x0_0_0x0_0_0 | pad | bytes 1572868 | tf_op jit(solution)/shard_map/pad | solution.py:57
  41.0 3.1 %convolution_bitcast_fusion.4 = f32[1,3,256,256]{3,2,1,0:T(8,128)} fusion(f32[1,4,256,256]{3,2,1,0:T(8,128)} %pad.79, f32[1,4,256,256]{3,2,1,0:T(8,128)S(1)} %pad.78, f32[1,8,256,256]{3,2,1,0:T(8,128)S(1)} %get-tuple-element.325), kind=kOutput, calls=%fused_computation.38 | convolution fusion | flops 604176384 | bytes 3145728 | tf_op jit(solution)/shard_map/...ij,...jk->...ik/dot_general | solution.py:33
  45.2 2.3 slice.227
  47.5 3.4 %convolution_bitcast_fusion.1 = f32[1,4,256,256]{3,2,1,0:T(8,128)S(1)} fusion(f32[1,4,256,256]{2,3,1,0:T(8,128)} %slice.227, f32[1,4,256,256]{2,3,1,0:T(8,128)} %copy-done.3), kind=kOutput, calls=%fused_computation.35 | convolution fusion | flops 805306368 | bytes 3145728 | tf_op jit(solution)/shard_map/...ij,...jk->...ik/dot_general | solution.py:33
  53.0 2.1 slice.223
  56.0 2.3 pad_maximum_fusion
  58.3 2.2 pad.80
  60.5 4.7 %pad.81 = f32[1,8,256,256]{3,2,1,0:T(8,128)} pad(f32[1,4,256,256]{3,2,1,0:T(8,128)} %add.246, f32[]{:T(128)} %constant.88.clone.1), padding=0_0_0x1_0_1x0_0_0x0_0_0 | pad | bytes 3145732 | tf_op jit(solution)/shard_map/pad | solution.py:57
  65.2 1.7 slice_add_fusion.1
  67.1 1.7 fusion.50
  72.8 1.2 pad.91
  74.0 1.1 add.259
  75.1 1.4 convolution_bitcast_fusion.3
  77.6 2.2 pad.92
  79.8 3.0 %pad.93 = f32[1,8,256,256]{3,2,1,0:T(8,128)} pad(f32[1,4,256,256]{3,2,1,0:T(8,128)S(1)} %copy-done.8, f32[]{:T(128)} %constant.88.clone.1), padding=0_0_0x1_0_1x0_0_0x0_0_0 | pad | bytes 3145732 | tf_op jit(solution)/shard_map/pad | solution.py:60
  82.8 3.3 %add.260 = f32[1,8,256,256]{3,2,1,0:T(8,128)} add(f32[1,8,256,256]{3,2,1,0:T(8,128)S(1)} %pad.92, f32[1,8,256,256]{3,2,1,0:T(8,128)} %pad.93) | non-fusion elementwise | flops 524288 | bytes 6291456 | tf_op jit(solution)/shard_map/add | solution.py:60
  86.1 3.1 %rev.12 = f32[1,8,256,256]{3,2,1,0:T(8,128)} reverse(f32[1,8,256,256]{3,2,1,0:T(8,128)} %add.260), dimensions={1} | reverse | bytes 4194304 | tf_op jit(solution)/shard_map/jit(_flip)/rev | solution.py:63
  89.2 9.1 %all_gather.13 = f32[4,1,256]{2,1,0:T(1,128)S(1)} all-gather(f32[1,1,256]{2,1,0:T(1,128)S(1)} %slice_add_fusion.3), channel_id=1, replica_groups=mesh['grp'=2,'step'=4,'chain'=2,'rep'=2] {'step'}, dimensions={0}, use_global_device_ids=true | all-gather | bytes 5120 | tf_op jit(solution)/shard_map/all_gather | solution.py:15
  98.3 8.3 %all_gather.15 = f32[4,1,256]{2,1,0:T(1,128)S(1)} all-gather(f32[1,1,256]{2,1,0:T(1,128)S(1)} %slice_add_fusion.2), channel_id=1, replica_groups=mesh['grp'=2,'step'=4,'chain'=2,'rep'=2] {'step'}, dimensions={0}, use_global_device_ids=true | all-gather | bytes 5120 | tf_op jit(solution)/shard_map/all_gather | solution.py:15
  106.5 1.7 slice_add_fusion
  108.4 11.0 %while.33 = (s32[]{:T(128)}, f32[1,256,256]{2,1,0:T(8,128)S(1)}, f32[1,256]{1,0:T(1,128)S(1)}, s32[]{:T(128)}, f32[4,1,256,256]{3,2,1,0:T(8,128)}, /*index=5*/f32[4,1,256]{2,1,0:T(1,128)S(1)}, s32[]{:T(128)}, s32[]{:T(128)}) while((s32[]{:T(128)}, f32[1,256,256]{2,1,0:T(8,128)S(1)}, f32[1,256]{1,0:T(1,128)S(1)}, s32[]{:T(128)}, ...), condition=%wide.region_1.2_spmd.clone, body=%wide.region_0.1_spmd.clone.sunk | while | flops 202179584 | bytes 1845375 | solution.py:26
  108.4 1.3 fusion.138
  109.8 1.3 fusion.137
  111.2 1.2 fusion.138
  112.5 1.3 fusion.137
  113.9 1.2 fusion.138
  115.3 1.3 fusion.137
  116.7 1.2 fusion.138
  118.0 1.3 fusion.137
  120.4 3.5 %fusion.19 = f32[1,8,256]{2,0,1:T(1,128)S(1)} fusion(f32[256,1,1]{0,1,2:T(1,128)S(1)} %fusion.28, f32[1,8,256,256]{3,2,1,0:T(8,128)S(1)} %copy-done.2, f32[1,8,256,256]{3,2,1,0:T(8,128)} %pad.81), kind=kOutput, calls=%fused_computation.27 | convolution fusion | flops 6815744 | bytes 4203520 | tf_op jit(solution)/shard_map/ctij,cj->cti/dot_general | solution.py:74
  123.9 11.5 %all-gather.5.cloned.1.call-done = f32[4,1,256,256]{3,2,1,0:T(8,128)} async-done(((f32[1,1,256,256]{3,2,1,0:T(8,128)}), f32[4,1,256,256]{3,2,1,0:T(8,128)}) %all-gather.5.cloned.1.call-update) | async-done | bytes 1048592 | tf_op jit(solution)/shard_map/all_gather | solution.py:15
  135.4 5.3 %while.34 = (s32[]{:T(128)}, f32[1,256]{1,0:T(1,128)S(1)}, s32[]{:T(128)}, f32[4,1,256,256]{3,2,1,0:T(8,128)}, f32[4,1,256]{2,1,0:T(1,128)S(1)}, /*index=5*/s32[]{:T(128)}, s32[]{:T(128)}, s32[]{:T(128)}, s32[]{:T(128)}) while((s32[]{:T(128)}, f32[1,256]{1,0:T(1,128)S(1)}, s32[]{:T(128)}, f32[4,1,256,256]{3,2,1,0:T(8,128)}, ...), condition=%wide.region_3.4_spmd.clone, body=%wide.region_2.3_spmd.clone.sunk | while | flops 787464 | bytes 272560 | solution.py:26
  135.4 1.2 fusion.141
  136.7 1.2 fusion.141
  138.1 1.2 fusion.141
  139.4 1.2 fusion.141
  140.7 3.4 %fusion.17 = f32[1,8,256]{2,0,1:T(1,128)S(1)} fusion(f32[1,8,256,256]{3,2,1,0:T(8,128)} %rev.12, f32[1,256]{1,0:T(1,128)S(1)} %get-tuple-element.247), kind=kOutput, calls=%fused_computation.25 | convolution fusion | flops 6291456 | bytes 2106368 | tf_op jit(solution)/shard_map/ctij,cj->cti/dot_general | solution.py:75
  144.2 32.4 %psum.15 = f32[256]{0:T(256)} all-reduce(f32[256]{0:T(256)S(1)} %broadcast_multiply_fusion), channel_id=1, replica_groups=mesh['grp'=2,'step'=4,'chain'=2,'rep'=2] {'step','chain','rep'}, use_global_device_ids=true, to_apply=%region_6.7 | all-reduce | flops 256 | bytes 2048 | tf_op jit(solution)/shard_map/psum | solution.py:81
  178.4 85.6 %all-reduce.26.cloned.1.call-done = f32[256,256]{1,0:T(8,128)} async-done(((f32[256,256]{1,0:T(8,128)}), f32[256,256]{1,0:T(8,128)}) %all-reduce.26.cloned.1.call-update) | async-done | bytes 262160 | tf_op jit(solution)/shard_map/psum | solution.py:81
  264.0 1.7 copy.83
  (163 shorter events, 24.5 us)
Async XLA Ops:
  7.2 15.2 %copy-start.9 = (f32[256,256]{1,0:T(8,128)S(1)}, f32[256,256]{1,0:T(8,128)}, u32[]{:S(2)}) copy-start(f32[256,256]{1,0:T(8,128)} %param.17) | copy-start | bytes 786436
  7.2 101.2 %all-gather.3.cloned.1.call-start = ((), (), s32[]{:S(2)}) async-start(), calls=%async_computation | async-start | bytes 1310720 | tf_op jit(solution)/shard_map/all_gather | solution.py:15
  8.0 9.1 %collective-permute-start = (f32[1,256]{1,0:T(1,128)S(1)}, f32[1,256]{1,0:T(1,128)S(1)}, u32[]{:S(2)}, u32[]{:S(2)}) collective-permute-start(f32[1,256]{1,0:T(1,128)S(1)} %slice_bitcast_fusion.12), channel_id=1, source_target_pairs={{0,4},{4,8},{8,12},{1,5},{5,9},{9,13},{2,6},{6,10},{10,14},{3,7},{... | collective-permute-start | bytes 3080 | tf_op jit(solution)/shard_map/ppermute | solution.py:10
  25.1 9.1 %copy-start.12 = (f32[1,4,256]{2,1,0:T(4,128)}, f32[1,4,256]{2,1,0:T(4,128)S(1)}, u32[]{:S(2)}) copy-start(f32[1,4,256]{2,1,0:T(4,128)S(1)} %bitcast_add_fusion.3) | copy-start | bytes 12292
  25.1 2.8 %copy-start = (f32[1,8,256,256]{2,3,1,0:T(8,128)S(1)}, f32[1,8,256,256]{2,3,1,0:T(8,128)}, u32[]{:S(2)}) copy-start(f32[1,8,256,256]{2,3,1,0:T(8,128)} %get-tuple-element.324) | copy-start | bytes 6291460
  30.7 1.9 copy-start.3
  31.4 21.2 %copy-start.11 = (f32[1,4,256]{2,1,0:T(4,128)}, f32[1,4,256]{2,1,0:T(4,128)S(1)}, u32[]{:S(2)}) copy-start(f32[1,4,256]{2,1,0:T(4,128)S(1)} %bitcast_add_fusion.1) | copy-start | bytes 12292
  41.0 3.1 %copy-start.4 = (f32[1,4,256,256]{3,2,1,0:T(8,128)S(1)}, f32[1,4,256,256]{3,2,1,0:T(8,128)}, u32[]{:S(2)}) copy-start(f32[1,4,256,256]{3,2,1,0:T(8,128)} %pad.79) | copy-start | bytes 3145732
  50.9 4.3 %slice-start.1 = ((f32[1,4,256]{2,1,0:T(4,128)}), f32[1,1,256]{2,1,0:T(1,128)S(1)}, s32[]{:S(2)}) async-start(f32[1,4,256]{2,1,0:T(4,128)} %copy-done.12), calls=%async_computation.4 | async-start | bytes 2048 | tf_op jit(solution)/shard_map/slice | solution.py:57
  51.6 0.8 copy-start.6
  60.4 6.5 %copy-start.1 = (f32[1,8,256,256]{3,2,1,0:T(8,128)}, f32[1,8,256,256]{3,2,1,0:T(8,128)S(1)}, u32[]{:S(2)}) copy-start(f32[1,8,256,256]{3,2,1,0:T(8,128)S(1)} %pad.80) | copy-start | bytes 6291460
  60.5 6.5 %slice-start = ((f32[1,4,256]{2,1,0:T(4,128)}), f32[1,1,256]{2,1,0:T(1,128)S(1)}, s32[]{:S(2)}) async-start(f32[1,4,256]{2,1,0:T(4,128)} %copy-done.11), calls=%async_computation.3 | async-start | bytes 2048 | tf_op jit(solution)/shard_map/slice | solution.py:60
  66.9 68.5 %all-gather.5.cloned.1.call-start = ((), (), s32[]{:S(2)}) async-start(), calls=%async_computation.1 | async-start | bytes 1310720 | tf_op jit(solution)/shard_map/all_gather | solution.py:15
  67.0 2.8 %copy-start.7 = (f32[1,2,256,256]{3,2,1,0:T(8,128)S(1)}, f32[1,2,256,256]{3,2,1,0:T(8,128)}, u32[]{:S(2)}) copy-start(f32[1,2,256,256]{3,2,1,0:T(8,128)} %copy-done.6) | copy-start | bytes 1572868
  72.8 2.4 copy-start.5
  75.1 1.4 copy-start.10
  77.6 2.3 copy-start.8
  108.3 12.1 %copy-start.2 = (f32[1,8,256,256]{3,2,1,0:T(8,128)S(1)}, f32[1,8,256,256]{3,2,1,0:T(8,128)}, u32[]{:S(2)}) copy-start(f32[1,8,256,256]{3,2,1,0:T(8,128)} %copy-done.1) | copy-start | bytes 6291460
  108.3 155.7 %all-reduce.26.cloned.1.call-start = ((), (), s32[]{:S(2)}) async-start(), calls=%async_computation.2 | async-start | bytes 524288 | tf_op jit(solution)/shard_map/psum | solution.py:81
  123.9 20.3 %copy-start.14 = (f32[1,8,256]{2,1,0:T(8,128)S(1)}, f32[1,8,256]{2,1,0:T(8,128)}, u32[]{:S(2)}) copy-start(f32[1,8,256]{2,1,0:T(8,128)} %param.21) | copy-start | bytes 24580
  123.9 20.3 %copy-start.15 = (f32[256]{0:T(256)S(1)}, f32[256]{0:T(256)}, u32[]{:S(2)}) copy-start(f32[256]{0:T(256)} %param.18) | copy-start | bytes 3076
  123.9 52.7 %copy-start.13 = (f32[1,8,256]{2,1,0:T(8,128)S(1)}, f32[1,8,256]{2,1,0:T(8,128)}, u32[]{:S(2)}) copy-start(f32[1,8,256]{2,1,0:T(8,128)} %param.20) | copy-start | bytes 24580
Sparse Core Ops, SparseCore 0:
  67.0 28.2 all-gather.2
  108.4 26.9 all-gather.4
  177.9 86.0 all-reduce.25
where the time goes:
time: 274 us; the launch traced here: 272 us
  waiting for transfers between devices  97.2 us (35%)
  blocking collectives  49.8 us (18%)
  matrix products  46 us (17%)
  local copies, waits for them, and re-layouts  38.7 us (14%)
  other arithmetic  19.8 us (7%)
  between operations  15 us (5%)
  starting transfers between devices  5.04 us (2%)
    psum x1, waiting for transfers between devices, shards(): lax.psum((grad_local, bias_local), ('step', 'chain', 'rep'))  85.6 us
    psum x1, blocking collectives, shards(): lax.psum((grad_local, bias_local), ('step', 'chain', 'rep'))  32.4 us
    all_gather x2, blocking collectives, carried_in(): everything = jax.tree.map(lambda part: lax.all_gather(part, axis), x)  17.4 us
    dot_general x14, matrix products, compose(): jnp.einsum('...ij,...jk->...ik', late_mat, early_mat, precision=highest)  17.2 us
    dot_general x18, matrix products, compose(): jnp.einsum('...ij,...j->...i', late_mat, early_vec, precision=highest)  16.1 us
    all_gather x2, waiting for transfers between devices, carried_in(): everything = jax.tree.map(lambda part: lax.all_gather(part, axis), x)  11.5 us
    slice x18, local copies, waits for them, and re-layouts, shards(): lax.associative_scan(compose, (jnp.flip(transposed, 1), jnp.flip(source,...  11.3 us
    pad x8, local copies, waits for them, and re-layouts, shards(): lax.associative_scan(compose, (jacobian, offset), axis=1)  10.9 us
  transfers between devices with their start and end apart: 4, of which 2 were waited for; matrix products, arithmetic and copies ran while one was open for 16% of the time, Pallas kernels for 0%

commit v1 on v0

v1 whole, which is shorter than its diff:
```python
import functools

import jax
import jax.numpy as jnp
from jax import lax
from jax.experimental import pallas as pl
from jax.experimental.pallas import tpu as pltpu
from jax.sharding import PartitionSpec as P

F32 = jnp.float32
BF16 = jnp.bfloat16
MESH = pl.DeviceIdType.MESH


def split(x):
    high = x.astype(BF16)
    return high, (x - high.astype(F32)).astype(BF16)


def rows_to_block(rows, steps, width):
    row = lax.broadcasted_iota(jnp.int32, (steps, width), 0)
    block = jnp.zeros((steps, width), F32)
    for t, value in rows.items():
        block = jnp.where(row == t, value, block)
    return block


def kernel(
    sizes, step_size,
    seed_ref, index_ref, init_ref, noise_ref, weight_ref, bias_ref, rates_ref, old_ref, cot_ref,
    path_ref, gw_ref, gb_ref,
    noise_v, maps, off_cols, cot_cols, edge_in, fwd_in, bwd_in, fwd_out, bwd_out,
    all_prev, all_weighted, slope_v,
    noise_sem, edge_send, edge_recv, fwd_send, fwd_recv, bwd_send, bwd_recv,
    prev_send, prev_recv, weighted_send, weighted_recv,
):
    ranks, chains, reps = sizes
    peers = ranks * chains * reps
    steps, width = old_ref.shape
    half = width // 2
    s, c, r = lax.axis_index("step"), lax.axis_index("chain"), lax.axis_index("rep")
    me = (s * chains + c) * reps + r

    def peer(d):
        other = lax.rem(me + d, peers)
        return {
            "step": other // (chains * reps),
            "chain": lax.rem(other // reps, chains),
            "rep": lax.rem(other, reps),
        }

    def each_peer(body):
        if peers <= 32:
            for d in range(1, peers):
                body(d)
        else:
            def one(d, carry):
                body(d)
                return carry
            lax.fori_loop(1, peers, one, 0)

    pieces = noise_sem.shape[0]
    piece = noise_ref.shape[0] // pieces
    loads = [
        pltpu.make_async_copy(
            noise_ref.at[pl.ds(k * piece, piece)], noise_v.at[pl.ds(k * piece, piece)], noise_sem.at[k]
        )
        for k in range(pieces)
    ]
    for load in loads:
        load.start()

    barrier = pltpu.get_barrier_semaphore()
    each_peer(
        lambda d: pl.semaphore_signal(barrier, inc=1, device_id=peer(d), device_id_type=MESH)
    )

    weight = weight_ref[...]
    weight_t = weight.T
    w_high, w_low = split(weight_t)
    pl.semaphore_wait(barrier, peers - 1)

    edge = pltpu.make_async_remote_copy(
        src_ref=old_ref.at[pl.ds(steps - 1, 1)], dst_ref=edge_in, send_sem=edge_send,
        recv_sem=edge_recv, device_id={"step": lax.rem(s + 1, ranks)}, device_id_type=MESH,
    )

    @pl.when(s < ranks - 1)
    def _():
        edge.start()

    start = init_ref[pl.ds(seed_ref[0], 1), :]
    for load in loads:
        load.wait()
    row = lax.broadcasted_iota(jnp.int32, (steps, width), 0)
    noise = jnp.concatenate([noise_v[pl.ds(index_ref[0, t], 1), :] for t in range(steps)], 0)

    @pl.when(s > 0)
    def _():
        edge.wait_recv()

    @pl.when(s == 0)
    def _():
        edge_in[...] = start

    first = edge_in[...]
    previous = jnp.concatenate([first, old_ref[0 : steps - 1, :]], 0)
    all_prev[0] = previous

    def prev_copy(d):
        return pltpu.make_async_remote_copy(
            src_ref=all_prev.at[0], dst_ref=all_prev.at[d], send_sem=prev_send.at[d],
            recv_sem=prev_recv.at[d], device_id=peer(d), device_id_type=MESH,
        )

    def weighted_copy(d):
        return pltpu.make_async_remote_copy(
            src_ref=all_weighted.at[0], dst_ref=all_weighted.at[d], send_sem=weighted_send.at[d],
            recv_sem=weighted_recv.at[d], device_id=peer(d), device_id_type=MESH,
        )

    def dot(a, b):
        return jnp.dot(a, b, preferred_element_type=F32)

    p_high, p_low = split(previous)
    mixed = dot(p_high, w_high) + (dot(p_low, w_high) + dot(p_high, w_low))
    squash = jnp.tanh(mixed + bias_ref[...] + noise)
    slope = 1.0 - squash * squash
    slope_v[...] = slope
    offset = step_size * (squash - slope * mixed)
    scaled = step_size * slope
    keep = 1.0 - rates_ref[...]
    cot = cot_ref[...]
    stacked = jnp.concatenate([scaled, offset, cot, jnp.zeros((128 - 3 * steps, width), F32)], 0)
    columns = stacked.T
    lane = lax.broadcasted_iota(jnp.int32, (width, 128), 1)
    diagonal = lax.broadcasted_iota(jnp.int32, (width, width), 0) == lax.broadcasted_iota(
        jnp.int32, (width, width), 1
    )
    for t in range(steps):
        kept = jnp.where(diagonal, keep[t : t + 1], 0.0)
        if t % 2 == 0:
            maps[t] = weight * columns[:, t : t + 1] + kept
            off_cols[t // 2] = jnp.where(lane == steps + t, columns, 0.0)
            cot_cols[t // 2] = jnp.where(lane == 2 * steps + t, columns, 0.0)
        else:
            maps[t] = weight_t * scaled[t : t + 1] + kept

    def to_column(t, x, extra):
        part = maps[t, :, :half] * x[:, :half] + maps[t, :, half:] * x[:, half:]
        return jnp.sum(part + extra, axis=1, keepdims=True)

    def to_row(t, x):
        return jnp.sum(maps[t] * x, axis=0, keepdims=True)

    def gather_columns(cols):
        total = jnp.zeros((width, 128), F32)
        for t, value in cols.items():
            total = jnp.where(lane == t, value, total)
        return total.T[0:steps]

    forward = pltpu.make_async_remote_copy(
        src_ref=fwd_out, dst_ref=fwd_in, send_sem=fwd_send, recv_sem=fwd_recv,
        device_id={"step": lax.rem(s + 1, ranks)}, device_id_type=MESH,
    )
    backward = pltpu.make_async_remote_copy(
        src_ref=bwd_out, dst_ref=bwd_in, send_sem=bwd_send, recv_sem=bwd_recv,
        device_id={"step": lax.rem(s + ranks - 1, ranks)}, device_id_type=MESH,
    )

    def run_forward():
        @pl.when(s == 0)
        def _():
            fwd_in[...] = start

        @pl.when(s > 0)
        def _():
            forward.wait_recv()

        x = fwd_in[...]
        rows, cols = {}, {}
        for t in range(steps):
            if t % 2 == 0:
                x = to_column(t, x, off_cols[t // 2])
                cols[t] = x
            else:
                x = to_row(t, x) + offset[t : t + 1]
                rows[t] = x
        fwd_out[...] = x

        @pl.when(s < ranks - 1)
        def _():
            forward.start()

        path_ref[...] = jnp.where(
            row % 2 == 0, gather_columns(cols), rows_to_block(rows, steps, width)
        )

    def run_backward():
        @pl.when(s == ranks - 1)
        def _():
            bwd_in[...] = jnp.zeros((1, width), F32)

        @pl.when(s < ranks - 1)
        def _():
            backward.wait_recv()

        a = bwd_in[...] + cot[steps - 1 : steps]
        rows, cols = {steps - 1: a}, {}
        for t in range(steps - 1, 0, -1):
            if t % 2 == 1:
                a = to_column(t, a, cot_cols[(t - 1) // 2])
                cols[t - 1] = a
            else:
                a = to_row(t, a) + cot[t - 1 : t]
                rows[t - 1] = a
        bwd_out[...] = to_row(0, a)

        @pl.when(s > 0)
        def _():
            backward.start()

        adjoint = jnp.where(
            row % 2 == 0, gather_columns(cols), rows_to_block(rows, steps, width)
        )
        all_weighted[0] = adjoint * slope_v[...]
        each_peer(lambda d: weighted_copy(d).start())

    early = s < ranks // 2

    @pl.when(early)
    def _():
        run_forward()
        each_peer(lambda d: prev_copy(d).start())
        run_backward()

    @pl.when(jnp.logical_not(early))
    def _():
        run_backward()
        each_peer(lambda d: prev_copy(d).start())
        run_forward()

    each_peer(lambda d: prev_copy(d).wait_recv())
    left = all_prev[...].reshape(peers * steps, width)
    l_high, l_low = split(left)
    each_peer(lambda d: weighted_copy(d).wait_recv())
    total = all_weighted[...].reshape(peers * steps, width)
    t_high, t_low = split(total)
    dims = (((0,), (0,)), ((), ()))

    def outer(a, b):
        return lax.dot_general(a, b, dims, preferred_element_type=F32)

    gw_ref[...] = step_size * (
        outer(t_high, l_high) + (outer(t_low, l_high) + outer(t_high, l_low))
    )
    gb_ref[...] = step_size * jnp.sum(total, axis=0, keepdims=True)

    each_peer(lambda d: prev_copy(d).wait_send())
    each_peer(lambda d: weighted_copy(d).wait_send())

    @pl.when(s < ranks - 1)
    def _():
        edge.wait_send()
        forward.wait_send()

    @pl.when(s > 0)
    def _():
        backward.wait_send()


def shards(sizes, seed, index, init_table, noise_table, weight, bias, rates, old_path, cotangent):
    ranks, chains, reps = sizes
    peers = ranks * chains * reps
    _, steps, width = old_path.shape
    vmem = pl.BlockSpec(memory_space=pltpu.VMEM)
    smem = pl.BlockSpec(memory_space=pltpu.SMEM)
    dma = pltpu.SemaphoreType.DMA
    path, grad_w, grad_b = pl.pallas_call(
        functools.partial(kernel, sizes, 4.0 / (steps * ranks)),
        out_shape=(
            jax.ShapeDtypeStruct((steps, width), F32),
            jax.ShapeDtypeStruct((width, width), F32),
            jax.ShapeDtypeStruct((1, width), F32),
        ),
        in_specs=[smem, smem, vmem, pl.BlockSpec(memory_space=pl.ANY)] + [vmem] * 5,
        out_specs=(vmem, vmem, vmem),
        scratch_shapes=[
            pltpu.VMEM(noise_table.shape, F32),
            pltpu.VMEM((steps, width, width), F32),
            pltpu.VMEM((steps // 2, width, 128), F32),
            pltpu.VMEM((steps // 2, width, 128), F32),
            pltpu.VMEM((1, width), F32),
            pltpu.VMEM((1, width), F32),
            pltpu.VMEM((1, width), F32),
            pltpu.VMEM((1, width), F32),
            pltpu.VMEM((1, width), F32),
            pltpu.VMEM((peers, steps, width), F32),
            pltpu.VMEM((peers, steps, width), F32),
            pltpu.VMEM((steps, width), F32),
            dma((8,)),
            dma, dma, dma, dma, dma, dma,
            dma((peers,)), dma((peers,)), dma((peers,)), dma((peers,)),
        ],
        compiler_params=pltpu.CompilerParams(
            collective_id=0, has_side_effects=True, vmem_limit_bytes=40 * 1024 * 1024
        ),
    )(
        seed, index, init_table, noise_table, weight, bias.reshape(1, width), rates,
        old_path.reshape(steps, width), cotangent.reshape(steps, width),
    )
    return path.reshape(1, steps, width), grad_w, grad_b.reshape(width)


def solution(mesh):
    sizes = (mesh.shape["step"], mesh.shape["chain"], mesh.shape["rep"])
    across = ("grp", "chain", "rep")
    placed = (
        P(across), P(across, "step"), P(), P(), P(), P(), P(("grp", "step"), None),
        P(across, "step", None), P(across, "step", None),
    )
    return jax.shard_map(
        functools.partial(shards, sizes),
        mesh=mesh,
        in_specs=placed,
        out_specs=(P(across, "step", None), P("grp", None), P("grp")),
        check_vma=False,
    )
```

time: 274 us -> 33.5 us (0.12)
  waiting for transfers between devices: 97.2 us -> 0 us
  blocking collectives: 49.8 us -> 0 us
  matrix products: 46 us -> 0 us
  local copies, waits for them, and re-layouts: 38.7 us -> 9.26 us
  Pallas kernels: 0 us -> 22.6 us
  other arithmetic: 19.8 us -> 0 us
  between operations: 15 us -> 1.3 us
  starting transfers between devices: 5.04 us -> 0 us
    psum x1 -> x0, waiting for transfers between devices: 85.6 us -> none  [shards(): lax.psum((grad_local, bias_local), ('step', 'chain', 'rep'))]
    dot_general x38 -> x0, matrix products: 46 us -> none  [the longest x14 17.2 us: compose(): jnp.einsum('...ij,...jk->...ik', late_mat, early_mat, precision=highest)]
    psum x1 -> x0, blocking collectives: 32.4 us -> none  [shards(): lax.psum((grad_local, bias_local), ('step', 'chain', 'rep'))]
    pallas_call x0 -> x1, Pallas kernels: none -> 22.6 us  [shards(): pl.pallas_call(functools.partial(kernel, sizes, 4.0 / (steps * ranks)), o...]
    pad x16 -> x0, local copies, waits for them, and re-layouts: 17.5 us -> none  [the longest x8 10.9 us: shards(): lax.associative_scan(compose, (jacobian, offset), axis=1)]
    all_gather x2 -> x0, blocking collectives: 17.4 us -> none  [carried_in(): everything = jax.tree.map(lambda part: lax.all_gather(part, axis), x)]
    slice x31 -> x0, local copies, waits for them, and re-layouts: 12.2 us -> none  [the longest x18 11.3 us: shards(): lax.associative_scan(compose, (jnp.flip(transposed, 1), jnp.flip(source,...]
    all_gather x2 -> x0, waiting for transfers between devices: 11.5 us -> none  [carried_in(): everything = jax.tree.map(lambda part: lax.all_gather(part, axis), x)]
  transfers between devices with their start and end apart: 4 -> 0, of which waited for: 2 -> 0; matrix products, arithmetic and copies ran while one was open for 16% -> 0% of each run, Pallas kernels for 0% -> 0%
where the time goes in v1:
time: 33.5 us; the launch traced here: 33.1 us
  Pallas kernels  22.6 us (67%)
  local copies, waits for them, and re-layouts  9.26 us (28%)
  between operations  1.3 us (4%)
    pallas_call x1, Pallas kernels, shards(): pl.pallas_call(functools.partial(kernel, sizes, 4.0 / (steps * ranks)), o...  22.6 us
    unnamed x19, local copies, waits for them, and re-layouts  9.26 us

profile of v1, /device:TPU:0, one launch (start us, length us, event | category | flops | bytes accessed | tf_op | source)
XLA Modules:
  0.0 33.1 jit_solution(15701146806174797786)
XLA Ops:
  1.3 0.0 copy-start
  1.3 2.2 %copy-done = f32[4096,256]{1,0:T(8,128)S(1)} copy-done((f32[4096,256]{1,0:T(8,128)S(1)}, f32[4096,256]{1,0:T(8,128)}, u32[]{:S(2)}) %copy-start) | copy-done | bytes 4194328
  3.5 0.0 copy-start.1
  3.5 0.9 %copy-done.1 = f32[256,256]{1,0:T(8,128)S(1)} copy-done((f32[256,256]{1,0:T(8,128)S(1)}, f32[256,256]{1,0:T(8,128)}, u32[]{:S(2)}) %copy-start.1) | copy-done | bytes 262168
  4.4 0.0 copy-start.2
  4.4 0.8 %copy-done.2 = f32[64,256]{1,0:T(8,128)S(1)} copy-done((f32[64,256]{1,0:T(8,128)S(1)}, f32[64,256]{1,0:T(8,128)}, u32[]{:S(2)}) %copy-start.2) | copy-done | bytes 65560
  5.3 0.0 copy-start.3
  5.3 0.7 %copy-done.3 = f32[8,256]{1,0:T(8,128)S(1)} copy-done((f32[8,256]{1,0:T(8,128)S(1)}, f32[8,256]{1,0:T(8,128)}, u32[]{:S(2)}) %copy-start.3) | copy-done | bytes 8216
  6.0 0.0 copy-start.4
  6.0 0.7 %copy-done.4 = f32[1,8,256]{2,1,0:T(8,128)S(1)} copy-done((f32[1,8,256]{2,1,0:T(8,128)S(1)}, f32[1,8,256]{2,1,0:T(8,128)}, u32[]{:S(2)}) %copy-start.4) | copy-done | bytes 8216
  6.7 0.0 copy-start.5
  6.7 0.7 %copy-done.5 = f32[1,8,256]{2,1,0:T(8,128)S(1)} copy-done((f32[1,8,256]{2,1,0:T(8,128)S(1)}, f32[1,8,256]{2,1,0:T(8,128)}, u32[]{:S(2)}) %copy-start.5) | copy-done | bytes 8216
  7.4 0.0 copy-start.6
  7.4 0.7 %copy-done.6 = f32[256]{0:T(256)S(1)} copy-done((f32[256]{0:T(256)S(1)}, f32[256]{0:T(256)}, u32[]{:S(2)}) %copy-start.6) | copy-done | bytes 1048
  8.0 0.0 copy-start.7
  8.0 0.7 %copy-done.7 = s32[1,8]{1,0:T(1,128)S(1)} copy-done((s32[1,8]{1,0:T(1,128)S(1)}, s32[1,8]{1,0:T(1,128)}, u32[]{:S(2)}) %copy-start.7) | copy-done | bytes 56
  8.7 22.6 %shard_map.112 = (f32[8,256]{1,0:T(8,128)S(1)}, f32[256,256]{1,0:T(8,128)S(1)}, f32[1,256]{1,0:T(1,128)S(1)}) custom-call(s32[1]{0:T(128)S(6)} %copy.15.seed_ref, s32[1,8]{1,0:T(1,128)S(1)} %copy-done.7, f32[64,256]{1,0:T(8,128)S(1)} %copy-done.2, f32[4096,256]{1,0:T(8,128)S(1)} %copy-done, f32[256,256]{1,0:T(8,128)S(1)} %copy-done.1, f32[1,256]{1,0:T(1,128)S(1)} %bitcast.9, ...), custom_call_target="tpu_custom_call" | custom-call | tf_op jit(solution)/shard_map/pallas_call | solution.py:279
  31.2 0.6 %copy.16 = f32[1,8,256]{2,1,0:T(8,128)} copy(f32[1,8,256]{2,1,0:T(8,128)S(1)} %bitcast.7) | data formatting | bytes 16384
  31.8 0.7 %copy.17 = f32[256,256]{1,0:T(8,128)} copy(f32[256,256]{1,0:T(8,128)S(1)} %get-tuple-element.13) | data formatting | bytes 524288
  32.5 0.6 %copy.18 = f32[256]{0:T(256)} copy(f32[256]{0:T(256)S(1)} %bitcast.8) | data formatting | bytes 2048
Async XLA Ops:
  1.3 2.2 %copy-start = (f32[4096,256]{1,0:T(8,128)S(1)}, f32[4096,256]{1,0:T(8,128)}, u32[]{:S(2)}) copy-start(f32[4096,256]{1,0:T(8,128)} %noise_ref.1) | copy-start | bytes 12582916
  3.5 0.9 %copy-start.1 = (f32[256,256]{1,0:T(8,128)S(1)}, f32[256,256]{1,0:T(8,128)}, u32[]{:S(2)}) copy-start(f32[256,256]{1,0:T(8,128)} %weight_ref.1) | copy-start | bytes 786436
  4.4 0.8 %copy-start.2 = (f32[64,256]{1,0:T(8,128)S(1)}, f32[64,256]{1,0:T(8,128)}, u32[]{:S(2)}) copy-start(f32[64,256]{1,0:T(8,128)} %init_ref.1) | copy-start | bytes 196612
  5.3 0.7 %copy-start.3 = (f32[8,256]{1,0:T(8,128)S(1)}, f32[8,256]{1,0:T(8,128)}, u32[]{:S(2)}) copy-start(f32[8,256]{1,0:T(8,128)} %rates_ref.1) | copy-start | bytes 24580
  6.0 0.7 %copy-start.4 = (f32[1,8,256]{2,1,0:T(8,128)S(1)}, f32[1,8,256]{2,1,0:T(8,128)}, u32[]{:S(2)}) copy-start(f32[1,8,256]{2,1,0:T(8,128)} %param.16) | copy-start | bytes 24580
  6.7 0.7 %copy-start.5 = (f32[1,8,256]{2,1,0:T(8,128)S(1)}, f32[1,8,256]{2,1,0:T(8,128)}, u32[]{:S(2)}) copy-start(f32[1,8,256]{2,1,0:T(8,128)} %param.17) | copy-start | bytes 24580
  7.4 0.7 %copy-start.6 = (f32[256]{0:T(256)S(1)}, f32[256]{0:T(256)}, u32[]{:S(2)}) copy-start(f32[256]{0:T(256)} %param.14) | copy-start | bytes 3076
  8.0 0.7 %copy-start.7 = (s32[1,8]{1,0:T(1,128)S(1)}, s32[1,8]{1,0:T(1,128)}, u32[]{:S(2)}) copy-start(s32[1,8]{1,0:T(1,128)} %index_ref.1) | copy-start | bytes 100

commit v2 on v1

--- a/solution.py
+++ b/solution.py
@@ -27,8 +27,9 @@
 
 def kernel(
     sizes, step_size,
-    seed_ref, index_ref, init_ref, noise_ref, weight_ref, bias_ref, rates_ref, old_ref, cot_ref,
+    seed_ref, index_ref, init_hbm, noise_ref, weight_hbm, bias_hbm, rates_hbm, old_hbm, cot_hbm,
     path_ref, gw_ref, gb_ref,
+    init_ref, weight_ref, bias_ref, rates_ref, old_ref, cot_ref, input_sem,
     noise_v, maps, off_cols, cot_cols, edge_in, fwd_in, bwd_in, fwd_out, bwd_out,
     all_prev, all_weighted, slope_v,
     noise_sem, edge_send, edge_recv, fwd_send, fwd_recv, bwd_send, bwd_recv,
@@ -59,6 +60,15 @@
                 return carry
             lax.fori_loop(1, peers, one, 0)
 
+    inputs = [
+        pltpu.make_async_copy(source, target, input_sem.at[k])
+        for k, (source, target) in enumerate((
+            (weight_hbm, weight_ref), (old_hbm, old_ref), (init_hbm, init_ref),
+            (bias_hbm, bias_ref), (rates_hbm, rates_ref), (cot_hbm, cot_ref),
+        ))
+    ]
+    for load in inputs:
+        load.start()
     pieces = noise_sem.shape[0]
     piece = noise_ref.shape[0] // pieces
     loads = [
@@ -75,6 +85,8 @@
         lambda d: pl.semaphore_signal(barrier, inc=1, device_id=peer(d), device_id_type=MESH)
     )
 
+    for load in inputs:
+        load.wait()
     weight = weight_ref[...]
     weight_t = weight.T
     w_high, w_low = split(weight_t)
@@ -283,9 +295,16 @@
             jax.ShapeDtypeStruct((width, width), F32),
             jax.ShapeDtypeStruct((1, width), F32),
         ),
-        in_specs=[smem, smem, vmem, pl.BlockSpec(memory_space=pl.ANY)] + [vmem] * 5,
+        in_specs=[smem, smem] + [pl.BlockSpec(memory_space=pltpu.HBM)] * 7,
         out_specs=(vmem, vmem, vmem),
         scratch_shapes=[
+            pltpu.VMEM(init_table.shape, F32),
+            pltpu.VMEM(weight.shape, F32),
+            pltpu.VMEM((1, width), F32),
+            pltpu.VMEM(rates.shape, F32),
+            pltpu.VMEM((steps, width), F32),
+            pltpu.VMEM((steps, width), F32),
+            dma((6,)),
             pltpu.VMEM(noise_table.shape, F32),
             pltpu.VMEM((steps, width, width), F32),
             pltpu.VMEM((steps // 2, width, 128), F32),
@@ -303,7 +322,7 @@
             dma((peers,)), dma((peers,)), dma((peers,)), dma((peers,)),
         ],
         compiler_params=pltpu.CompilerParams(
-            collective_id=0, has_side_effects=True, vmem_limit_bytes=40 * 1024 * 1024
+            collective_id=0, has_side_effects=True, vmem_limit_bytes=64 * 1024 * 1024 - 4096
         ),
     )(
         seed, index, init_table, noise_table, weight, bias.reshape(1, width), rates,

time: 33.5 us -> 29.1 us (0.87)
  local copies, waits for them, and re-layouts: 9.26 us -> 4.19 us
  Pallas kernels: 22.6 us -> 23.4 us
    unnamed x19 -> x3, local copies, waits for them, and re-layouts: 9.26 us -> 4.19 us
    pallas_call x1, Pallas kernels: 22.6 us -> 23.4 us  [shards(): pl.pallas_call(functools.partial(kernel, sizes, 4.0 / (steps * ranks)), o...]
where the time goes in v2:
time: 29.1 us; the launch traced here: 28.9 us
  Pallas kernels  23.4 us (80%)
  local copies, waits for them, and re-layouts  4.19 us (14%)
  between operations  1.29 us (4%)
    pallas_call x1, Pallas kernels, shards(): pl.pallas_call(functools.partial(kernel, sizes, 4.0 / (steps * ranks)), o...  23.4 us
    unnamed x3, local copies, waits for them, and re-layouts  4.19 us

profile of v2, /device:TPU:0, one launch (start us, length us, event | category | flops | bytes accessed | tf_op | source)
XLA Modules:
  0.0 28.9 jit_solution(18130167103843346458)
XLA Ops:
  1.3 23.4 %shard_map.112 = (f32[8,256]{1,0:T(8,128)}, f32[256,256]{1,0:T(8,128)}, f32[1,256]{1,0:T(1,128)}) custom-call(s32[1]{0:T(128)S(6)} %copy.15.seed_ref, s32[1,8]{1,0:T(1,128)} %index_ref.1, f32[64,256]{1,0:T(8,128)} %init_hbm.1, f32[4096,256]{1,0:T(8,128)} %noise_ref.1, f32[256,256]{1,0:T(8,128)} %weight_hbm.1, f32[1,256]{1,0:T(1,128)} %bitcast.9, ...), custom_call_target="tpu_custom_call" | custom-call | tf_op jit(solution)/shard_map/pallas_call | solution.py:291
  24.7 1.3 %copy.16 = f32[1,8,256]{2,1,0:T(8,128)} copy(f32[1,8,256]{2,1,0:T(8,128)} %bitcast.7) | data formatting | bytes 16384
  26.0 1.7 %copy.17 = f32[256,256]{1,0:T(8,128)} copy(f32[256,256]{1,0:T(8,128)} %get-tuple-element.13) | data formatting | bytes 524288
  27.6 1.2 %copy.18 = f32[256]{0:T(256)} copy(f32[256]{0:T(256)} %bitcast.8) | data formatting | bytes 2048

commit v3 on v2

--- a/solution.py
+++ b/solution.py
@@ -125,6 +125,8 @@
             recv_sem=prev_recv.at[d], device_id=peer(d), device_id_type=MESH,
         )
 
+    each_peer(lambda d: prev_copy(d).start())
+
     def weighted_copy(d):
         return pltpu.make_async_remote_copy(
             src_ref=all_weighted.at[0], dst_ref=all_weighted.at[d], send_sem=weighted_send.at[d],
@@ -243,13 +245,11 @@
     @pl.when(early)
     def _():
         run_forward()
-        each_peer(lambda d: prev_copy(d).start())
         run_backward()
 
     @pl.when(jnp.logical_not(early))
     def _():
         run_backward()
-        each_peer(lambda d: prev_copy(d).start())
         run_forward()
 
     each_peer(lambda d: prev_copy(d).wait_recv())

time: 29.1 us -> 29.5 us (1.014)
  Pallas kernels: 23.4 us -> 23.8 us
    pallas_call x1, Pallas kernels: 23.4 us -> 23.8 us  [shards(): pl.pallas_call(functools.partial(kernel, sizes, 4.0 / (steps * ranks)), o...]
where the time goes in v3:
time: 29.5 us; the launch traced here: 29.3 us
  Pallas kernels  23.8 us (81%)
  local copies, waits for them, and re-layouts  4.19 us (14%)
  between operations  1.29 us (4%)
    pallas_call x1, Pallas kernels, shards(): pl.pallas_call(functools.partial(kernel, sizes, 4.0 / (steps * ranks)), o...  23.8 us
    unnamed x3, local copies, waits for them, and re-layouts  4.19 us

profile of v3, /device:TPU:0, one launch (start us, length us, event | category | flops | bytes accessed | tf_op | source)
XLA Modules:
  0.0 29.3 jit_solution(15150084624753070081)
XLA Ops:
  1.3 23.8 %shard_map.112 = (f32[8,256]{1,0:T(8,128)}, f32[256,256]{1,0:T(8,128)}, f32[1,256]{1,0:T(1,128)}) custom-call(s32[1]{0:T(128)S(6)} %copy.15.seed_ref, s32[1,8]{1,0:T(1,128)} %index_ref.1, f32[64,256]{1,0:T(8,128)} %init_hbm.1, f32[4096,256]{1,0:T(8,128)} %noise_ref.1, f32[256,256]{1,0:T(8,128)} %weight_hbm.1, f32[1,256]{1,0:T(1,128)} %bitcast.9, ...), custom_call_target="tpu_custom_call" | custom-call | tf_op jit(solution)/shard_map/pallas_call | solution.py:291
  25.1 1.3 %copy.16 = f32[1,8,256]{2,1,0:T(8,128)} copy(f32[1,8,256]{2,1,0:T(8,128)} %bitcast.7) | data formatting | bytes 16384
  26.4 1.7 %copy.17 = f32[256,256]{1,0:T(8,128)} copy(f32[256,256]{1,0:T(8,128)} %get-tuple-element.13) | data formatting | bytes 524288
  28.0 1.2 %copy.18 = f32[256]{0:T(256)} copy(f32[256]{0:T(256)} %bitcast.8) | data formatting | bytes 2048

commit v4 on v2

--- a/solution.py
+++ b/solution.py
@@ -117,19 +117,57 @@
 
     first = edge_in[...]
     previous = jnp.concatenate([first, old_ref[0 : steps - 1, :]], 0)
-    all_prev[0] = previous
-
-    def prev_copy(d):
+    all_prev[0, 0] = previous
+
+    plane = chains * reps
+    mine = c * reps + r
+
+    def along_step(data, sends, recvs, k):
         return pltpu.make_async_remote_copy(
-            src_ref=all_prev.at[0], dst_ref=all_prev.at[d], send_sem=prev_send.at[d],
-            recv_sem=prev_recv.at[d], device_id=peer(d), device_id_type=MESH,
-        )
-
-    def weighted_copy(d):
+            src_ref=data.at[0, 0], dst_ref=data.at[0, k], send_sem=sends.at[k],
+            recv_sem=recvs.at[k],
+            device_id={"step": lax.rem(s + k, ranks)}, device_id_type=MESH,
+        )
+
+    def in_plane(data, sends, recvs, d, k):
+        other = lax.rem(mine + d, plane)
         return pltpu.make_async_remote_copy(
-            src_ref=all_weighted.at[0], dst_ref=all_weighted.at[d], send_sem=weighted_send.at[d],
-            recv_sem=weighted_recv.at[d], device_id=peer(d), device_id_type=MESH,
-        )
+            src_ref=data.at[0, k], dst_ref=data.at[d, k], send_sem=sends.at[d * ranks + k],
+            recv_sem=recvs.at[d * ranks + k],
+            device_id={"chain": other // reps, "rep": lax.rem(other, reps)}, device_id_type=MESH,
+        )
+
+    def send_own(group):
+        for k in range(1, ranks):
+            along_step(*group, k).start()
+        for d in range(1, plane):
+            in_plane(*group, d, 0).start()
+
+    def forward_block(group, k):
+        along_step(*group, k).wait_recv()
+        for d in range(1, plane):
+            in_plane(*group, d, k).start()
+
+    def forward_all(group):
+        for q in reversed(range(ranks)):
+            @pl.when(s != q)
+            def _():
+                forward_block(group, lax.rem(s - q + ranks, ranks))
+
+    def wait_plane(group):
+        for d in range(1, plane):
+            for k in range(ranks):
+                in_plane(*group, d, k).wait_recv()
+
+    def wait_sent(group):
+        for k in range(1, ranks):
+            along_step(*group, k).wait_send()
+        for d in range(1, plane):
+            for k in range(ranks):
+                in_plane(*group, d, k).wait_send()
+
+    prev_group = (all_prev, prev_send, prev_recv)
+    weighted_group = (all_weighted, weighted_send, weighted_recv)
 
     def dot(a, b):
         return jnp.dot(a, b, preferred_element_type=F32)
@@ -235,27 +273,29 @@
         adjoint = jnp.where(
             row % 2 == 0, gather_columns(cols), rows_to_block(rows, steps, width)
         )
-        all_weighted[0] = adjoint * slope_v[...]
-        each_peer(lambda d: weighted_copy(d).start())
+        all_weighted[0, 0] = adjoint * slope_v[...]
+        send_own(weighted_group)
 
     early = s < ranks // 2
 
     @pl.when(early)
     def _():
         run_forward()
-        each_peer(lambda d: prev_copy(d).start())
+        send_own(prev_group)
         run_backward()
 
     @pl.when(jnp.logical_not(early))
     def _():
         run_backward()
-        each_peer(lambda d: prev_copy(d).start())
+        send_own(prev_group)
         run_forward()
 
-    each_peer(lambda d: prev_copy(d).wait_recv())
+    forward_all(prev_group)
+    wait_plane(prev_group)
     left = all_prev[...].reshape(peers * steps, width)
     l_high, l_low = split(left)
-    each_peer(lambda d: weighted_copy(d).wait_recv())
+    forward_all(weighted_group)
+    wait_plane(weighted_group)
     total = all_weighted[...].reshape(peers * steps, width)
     t_high, t_low = split(total)
     dims = (((0,), (0,)), ((), ()))
@@ -268,8 +308,8 @@
     )
     gb_ref[...] = step_size * jnp.sum(total, axis=0, keepdims=True)
 
-    each_peer(lambda d: prev_copy(d).wait_send())
-    each_peer(lambda d: weighted_copy(d).wait_send())
+    wait_sent(prev_group)
+    wait_sent(weighted_group)
 
     @pl.when(s < ranks - 1)
     def _():
@@ -314,8 +354,8 @@
             pltpu.VMEM((1, width), F32),
             pltpu.VMEM((1, width), F32),
             pltpu.VMEM((1, width), F32),
-            pltpu.VMEM((peers, steps, width), F32),
-            pltpu.VMEM((peers, steps, width), F32),
+            pltpu.VMEM((chains * reps, ranks, steps, width), F32),
+            pltpu.VMEM((chains * reps, ranks, steps, width), F32),
             pltpu.VMEM((steps, width), F32),
             dma((8,)),
             dma, dma, dma, dma, dma, dma,

time: 29.1 us -> 32.6 us (1.12)
  Pallas kernels: 23.4 us -> 26.9 us
    pallas_call x1, Pallas kernels: 23.4 us -> 26.9 us  [shards(): pl.pallas_call(functools.partial(kernel, sizes, 4.0 / (steps * ranks)), o...]
where the time goes in v4:
time: 32.6 us; the launch traced here: 32.4 us
  Pallas kernels  26.9 us (83%)
  local copies, waits for them, and re-layouts  4.19 us (13%)
  between operations  1.29 us (4%)
    pallas_call x1, Pallas kernels, shards(): pl.pallas_call(functools.partial(kernel, sizes, 4.0 / (steps * ranks)), o...  26.9 us
    unnamed x3, local copies, waits for them, and re-layouts  4.19 us

profile of v4, /device:TPU:0, one launch (start us, length us, event | category | flops | bytes accessed | tf_op | source)
XLA Modules:
  0.0 32.4 jit_solution(5924097537856344535)
XLA Ops:
  1.3 26.9 %shard_map.112 = (f32[8,256]{1,0:T(8,128)}, f32[256,256]{1,0:T(8,128)}, f32[1,256]{1,0:T(1,128)}) custom-call(s32[1]{0:T(128)S(6)} %copy.15.seed_ref, s32[1,8]{1,0:T(1,128)} %index_ref.1, f32[64,256]{1,0:T(8,128)} %init_hbm.1, f32[4096,256]{1,0:T(8,128)} %noise_ref.1, f32[256,256]{1,0:T(8,128)} %weight_hbm.1, f32[1,256]{1,0:T(1,128)} %bitcast.9, ...), custom_call_target="tpu_custom_call" | custom-call | tf_op jit(solution)/shard_map/pallas_call | solution.py:331
  28.2 1.3 %copy.16 = f32[1,8,256]{2,1,0:T(8,128)} copy(f32[1,8,256]{2,1,0:T(8,128)} %bitcast.7) | data formatting | bytes 16384
  29.5 1.7 %copy.17 = f32[256,256]{1,0:T(8,128)} copy(f32[256,256]{1,0:T(8,128)} %get-tuple-element.13) | data formatting | bytes 524288
  31.2 1.2 %copy.18 = f32[256]{0:T(256)} copy(f32[256]{0:T(256)} %bitcast.8) | data formatting | bytes 2048

commit v5 on v2

--- a/solution.py
+++ b/solution.py
@@ -40,14 +40,15 @@
     steps, width = old_ref.shape
     half = width // 2
     s, c, r = lax.axis_index("step"), lax.axis_index("chain"), lax.axis_index("rep")
-    me = (s * chains + c) * reps + r
+
+    def wrap(x, size):
+        return jnp.where(x >= size, x - size, x)
 
     def peer(d):
-        other = lax.rem(me + d, peers)
         return {
-            "step": other // (chains * reps),
-            "chain": lax.rem(other // reps, chains),
-            "rep": lax.rem(other, reps),
+            "step": wrap(s + d // (chains * reps), ranks),
+            "chain": wrap(c + d // reps % chains, chains),
+            "rep": wrap(r + d % reps, reps),
         }
 
     def each_peer(body):

time: 29.1 us -> 29.1 us (level)
  no operation moved by 1% of the time
where the time goes in v5:
time: 29.1 us; the launch traced here: 28.8 us
  Pallas kernels  23.3 us (80%)
  local copies, waits for them, and re-layouts  4.19 us (14%)
  between operations  1.29 us (4%)
    pallas_call x1, Pallas kernels, shards(): pl.pallas_call(functools.partial(kernel, sizes, 4.0 / (steps * ranks)), o...  23.3 us
    unnamed x3, local copies, waits for them, and re-layouts  4.19 us

profile of v5, /device:TPU:0, one launch (start us, length us, event | category | flops | bytes accessed | tf_op | source)
XLA Modules:
  0.0 28.8 jit_solution(3892197703113079560)
XLA Ops:
  1.3 23.3 %shard_map.112 = (f32[8,256]{1,0:T(8,128)}, f32[256,256]{1,0:T(8,128)}, f32[1,256]{1,0:T(1,128)}) custom-call(s32[1]{0:T(128)S(6)} %copy.15.seed_ref, s32[1,8]{1,0:T(1,128)} %index_ref.1, f32[64,256]{1,0:T(8,128)} %init_hbm.1, f32[4096,256]{1,0:T(8,128)} %noise_ref.1, f32[256,256]{1,0:T(8,128)} %weight_hbm.1, f32[1,256]{1,0:T(1,128)} %bitcast.9, ...), custom_call_target="tpu_custom_call" | custom-call | tf_op jit(solution)/shard_map/pallas_call | solution.py:292
  24.6 1.3 %copy.16 = f32[1,8,256]{2,1,0:T(8,128)} copy(f32[1,8,256]{2,1,0:T(8,128)} %bitcast.7) | data formatting | bytes 16384
  25.9 1.7 %copy.17 = f32[256,256]{1,0:T(8,128)} copy(f32[256,256]{1,0:T(8,128)} %get-tuple-element.13) | data formatting | bytes 524288
  27.6 1.2 %copy.18 = f32[256]{0:T(256)} copy(f32[256]{0:T(256)} %bitcast.8) | data formatting | bytes 2048
